TPU v7x, 32 devices: a whole 2x2x4 slice. The times are simulated.
32 devices in a mesh: seq: 8 (over z, core), tensor: 4 (over y, x).
Axes of the slice: x: 2, y: 2, z: 4, core: 2. Of those that a mesh axis runs over, the one named last changes fastest.
Arguments:
- queries: bfloat16 [3, 24, 40, 5120], P(None, 'seq', None, 'tensor'), may hold values from -16 to 16
- keys_values: bfloat16 [2, 3, 24, 40, 5120], P(None, None, 'seq', None, 'tensor'), may hold values from -16 to 16
- out_weight: bfloat16 [5120, 5120], P('tensor'), may hold values from -0.078125 to 0.078125
- grad_out: bfloat16 [3, 24, 40, 5120], P(None, 'seq', 'tensor'), may hold values from -6 to 6
- window: int32 [40, 3], P('tensor'), may hold values from 0 to 3, as said below
- block_mask: int32 [1, 8, 5, 63], replicated, may hold values from 0 to 1, as said below
Outputs:
- layer_out: bfloat16 [3, 24, 40, 5120], P(None, 'seq', 'tensor')
- grad_queries: bfloat16 [3, 24, 40, 5120], P(None, 'seq', None, 'tensor')
- grad_keys_values: bfloat16 [2, 3, 24, 40, 5120], P(None, None, 'seq', None, 'tensor')
- grad_weight: bfloat16 [5120, 5120], P('tensor', 'seq')
Inputs may be any that keep to these rules, and one draw needn't show every extreme that they name: `window`: in every group of 10 consecutive heads one head has the reach (1, 1, 3). `block_mask`: the middle entry of every tile's row (the tile itself) is 1.
All inputs are finite; a program needn't handle non-finite values.
Results may differ from a plain program's by a relative error of at most 0.014.
Values may be sent and summed in bfloat16 or wider, within the bound.
A program may use at most 128 MiB of HBM per device.

v0:
```python
import jax
import jax.numpy as jnp
from jax import lax
from jax.experimental import pallas as pl
from jax.experimental.pallas import tpu as pltpu
from jax.sharding import PartitionSpec as P

HEAD_DIM = 128
TILE_F = 3
TILE_H = 3
TILE_W = 8
REACH_F = 1
REACH_H = 1
REACH_W = 3
OFFSETS = 63
SCALE = HEAD_DIM**-0.5
LOG2E = 1.4426950408889634
LANES = 128
BLOCKED = -1e30
F32 = jnp.float32
BF16 = jnp.bfloat16
NT = (((1,), (1,)), ((), ()))
TN = (((0,), (0,)), ((), ()))


def mm(left, right, dims=(((1,), (0,)), ((), ()))):
    return lax.dot_general(left, right, dims, preferred_element_type=F32)


def swap(value, axis, bit):
    count = lax.axis_size(axis)
    return lax.ppermute(value, axis, [(i, i ^ bit) for i in range(count)])


def shift(value, axis, steps):
    count = lax.axis_size(axis)
    pairs = [(i, i + steps) for i in range(count) if 0 <= i + steps < count]
    return lax.ppermute(value, axis, pairs)


def turn(value, axis, steps):
    count = lax.axis_size(axis)
    return lax.ppermute(value, axis, [(i, (i + steps) % count) for i in range(count)])


def weights_of(q_ref, bias_ref, place_ref, kv_refs, onehot_ref):
    q_rows = mm(place_ref[...], q_ref[...]).astype(BF16)
    q_wide = jnp.concatenate([q_rows, bias_ref[0]], axis=1)
    scores = [
        mm(jnp.concatenate([ref[0], onehot_ref[part]], axis=1), q_wide, NT)
        for part, ref in enumerate(kv_refs)
    ]
    return q_rows, scores


def forward_kernel(q_ref, own_ref, above_ref, below_ref, bias_ref, place_ref, onehot_ref, att_ref, stat_ref):
    kv_refs = (above_ref, own_ref, below_ref)
    _, scores = weights_of(q_ref, bias_ref, place_ref, kv_refs, onehot_ref)
    tops = [jnp.max(part, axis=0, keepdims=True) for part in scores]
    top = jnp.maximum(jnp.maximum(tops[0], tops[1]), tops[2]) * (SCALE * LOG2E)
    total = jnp.zeros_like(top)
    out = jnp.zeros((HEAD_DIM, top.shape[1]), F32)
    for part, ref in zip(scores, kv_refs):
        weights = jnp.exp2(part * (SCALE * LOG2E) - top)
        total = total + jnp.sum(weights, axis=0, keepdims=True)
        out = out + mm(ref[1], weights.astype(BF16), TN)
    inverse = 1.0 / total
    att_ref[...] = (out * inverse).T.astype(BF16)
    row = lax.broadcasted_iota(jnp.int32, (8, top.shape[1]), 0)
    stat_ref[0] = jnp.where(row == 0, top, inverse)


def backward_kernel(
    q_ref, own_ref, above_ref, below_ref, bias_ref, place_ref, onehot_ref, g_ref, stat_ref,
    dq_ref, down_ref, dabove_ref, dbelow_ref,
):
    kv_refs = (above_ref, own_ref, below_ref)
    q_rows, scores = weights_of(q_ref, bias_ref, place_ref, kv_refs, onehot_ref)
    top = stat_ref[0, 0:1, :]
    inverse = stat_ref[0, 1:2, :]
    columns = top.shape[1]
    g_scaled = (g_ref[...].astype(F32).T * inverse).astype(BF16)
    weights, rounded = [], []
    out = jnp.zeros((HEAD_DIM, columns), F32)
    for part, ref in zip(scores, kv_refs):
        value = jnp.exp2(part * (SCALE * LOG2E) - top)
        weights.append(value)
        rounded.append(value.astype(BF16))
        out = out + mm(ref[1], rounded[-1], TN)
    delta = jnp.sum(out * inverse * g_scaled.astype(F32), axis=0, keepdims=True)
    high = delta.astype(BF16).astype(F32)
    row = lax.broadcasted_iota(jnp.int32, (LANES, columns), 0)
    extra = jnp.where(row == 0, -high, jnp.where(row == 1, high - delta, 0.0)).astype(BF16)
    g_wide = jnp.concatenate([g_scaled, extra], axis=0)
    keys = own_ref.shape[1]
    pick = (lax.broadcasted_iota(jnp.int32, (keys, LANES), 1) < 2).astype(F32).astype(BF16)
    dq = jnp.zeros((HEAD_DIM, columns), F32)
    for index, (ref, target) in enumerate(zip(kv_refs, (dabove_ref, down_ref, dbelow_ref))):
        inner = mm(jnp.concatenate([ref[1], pick], axis=1), g_wide)
        slope = (weights[index] * inner).astype(BF16)
        target[1] = mm(rounded[index], g_scaled, NT).astype(target.dtype)
        target[0] = (mm(slope, q_rows) * SCALE).astype(target.dtype)
        dq = dq + mm(ref[0], slope, TN)
    dq_rows = (dq * SCALE).astype(BF16).T
    dq_ref[...] = mm(place_ref[...], dq_rows, TN).astype(BF16)


def tile_bias(window, mask_rows, row_place, row_tiles, column_tiles):
    query = jnp.arange(column_tiles, dtype=jnp.int32)[:, None]
    linear = jnp.arange(3 * column_tiles, dtype=jnp.int32)[None, :]
    delta_h = linear // column_tiles - 1
    delta_w = linear % column_tiles - query
    key_row = row_place + delta_h
    offset = (REACH_F * (2 * REACH_H + 1) + delta_h + REACH_H) * (2 * REACH_W + 1) + delta_w + REACH_W
    bits = jnp.sum(
        jnp.where(
            offset[:, :, None] == jnp.arange(OFFSETS, dtype=jnp.int32), mask_rows[:, None, :], 0
        ),
        axis=-1,
    )
    kept = (bits > 0) & (jnp.abs(delta_w) <= REACH_W) & (key_row >= 0) & (key_row < row_tiles)
    reach = window[:, :, None, None]
    kept = kept & (jnp.abs(delta_h) <= reach[:, 1]) & (jnp.abs(delta_w) <= reach[:, 2])
    kept = kept & (reach[:, 0] >= 0)
    return jnp.where(kept, 0.0, BLOCKED).astype(BF16)


def shards(queries, keys_values, out_weight, grad_out, window, block_mask):
    frames, tile_rows, columns, channels = queries.shape
    model_width = grad_out.shape[3]
    local_columns = grad_out.shape[2]
    seq_count, tensor_count = lax.axis_size("seq"), lax.axis_size("tensor")
    seq_place, tensor_place = lax.axis_index("seq"), lax.axis_index("tensor")
    chips = seq_count // 2
    chip, core = seq_place // 2, seq_place % 2
    heads = channels // HEAD_DIM
    tokens = frames * tile_rows * columns
    piece = frames * tile_rows * local_columns
    slab = -(-piece // 16) * 16
    rows = tensor_count * slab
    width = model_width // seq_count

    q_flat = queries.reshape(tokens, channels)
    kv_flat = keys_values.reshape(2, tokens, channels)
    kv_above = shift(kv_flat, "seq", 1)
    kv_below = shift(kv_flat, "seq", -1)

    g_own = jnp.pad(grad_out.reshape(piece, model_width), ((0, slab - piece), (0, 0)))
    g_all = jnp.concatenate(
        [g_own] + [swap(g_own, "tensor", bit) for bit in range(1, tensor_count)], axis=0
    )

    def columns_for(place):
        return lax.dynamic_slice_in_dim(g_own, place * 2 * width, 2 * width, axis=1)

    moved = jnp.stack(
        [columns_for(chip)]
        + [
            turn(columns_for(lax.rem(chip + k, chips)), "seq", 2 * k)
            for k in range(1, chips)
        ]
    )
    kept_half = lax.dynamic_slice_in_dim(moved, core * width, width, axis=2)
    sent_half = lax.dynamic_slice_in_dim(moved, (1 - core) * width, width, axis=2)
    pair = jnp.stack([kept_half, swap(sent_half, "seq", 1)], axis=1)
    pair_all = jnp.stack(
        [pair] + [swap(pair, "tensor", bit) for bit in range(1, tensor_count)], axis=2
    ).reshape(chips, 2 * rows, width)

    row_id = jnp.arange(rows, dtype=jnp.int32)
    owner = jnp.bitwise_xor(row_id // slab, tensor_place)
    inside = row_id % slab
    column_id = owner * local_columns + inside % local_columns
    token_id = jnp.where(inside < piece, inside // local_columns * columns + column_id, -1)
    place = (token_id[:, None] == jnp.arange(tokens, dtype=jnp.int32)[None, :]).astype(BF16)
    column_tiles = columns // TILE_W
    own_mask = lax.dynamic_slice_in_dim(block_mask, seq_place, 1, 1).reshape(-1, OFFSETS)
    bias = tile_bias(window, own_mask, seq_place, seq_count, column_tiles)
    bias = jnp.pad(bias, ((0, 0), (0, 0), (0, LANES - bias.shape[2])))
    query_tile = jnp.where(inside < piece, column_id // TILE_W, -1)
    row_bias = jnp.zeros((heads, rows, LANES), BF16)
    for tile in range(column_tiles):
        row_bias = jnp.where((query_tile == tile)[None, :, None], bias[:, tile][:, None, :], row_bias)
    key_tile = (
        jnp.arange(tokens, dtype=jnp.int32)[None, :] % columns // TILE_W
        + jnp.arange(3, dtype=jnp.int32)[:, None] * column_tiles
    )
    onehot = (key_tile[:, :, None] == jnp.arange(LANES, dtype=jnp.int32)).astype(BF16)

    q_spec = pl.BlockSpec((tokens, HEAD_DIM), lambda h: (0, h))
    kv_spec = pl.BlockSpec((2, tokens, HEAD_DIM), lambda h: (0, 0, h))
    bias_spec = pl.BlockSpec((1, rows, LANES), lambda h: (h, 0, 0))
    place_spec = pl.BlockSpec((rows, tokens), lambda h: (0, 0))
    onehot_spec = pl.BlockSpec((3, tokens, LANES), lambda h: (0, 0, 0))
    row_spec = pl.BlockSpec((rows, HEAD_DIM), lambda h: (0, h))
    stat_spec = pl.BlockSpec((1, 8, rows), lambda h: (h, 0, 0))
    common = (q_spec, kv_spec, kv_spec, kv_spec, bias_spec, place_spec, onehot_spec)
    params = pltpu.CompilerParams(vmem_limit_bytes=40 * 1024 * 1024)
    work = heads * rows * tokens * 3 * HEAD_DIM * 2
    size = tokens * channels * 2

    attended, stats = pl.pallas_call(
        forward_kernel,
        grid=(heads,),
        in_specs=list(common),
        out_specs=[row_spec, stat_spec],
        out_shape=[
            jax.ShapeDtypeStruct((rows, channels), BF16),
            jax.ShapeDtypeStruct((heads, 8, rows), F32),
        ],
        compiler_params=params,
        cost_estimate=pl.CostEstimate(flops=4 * work, bytes_accessed=9 * size, transcendentals=heads * rows * tokens * 3),
        name="forward",
    )(q_flat, kv_flat, kv_above, kv_below, row_bias, place, onehot)

    ups, downs = [attended], [attended]
    for _ in range(1, chips):
        ups.append(shift(ups[-1], "seq", 2))
        downs.append(shift(downs[-1], "seq", -2))
    chunks = [attended] + [ups[k] + downs[chips - k] for k in range(1, chips)]
    grad_weight = jnp.zeros((channels, width), F32)
    for k in range(chips):
        both = jnp.concatenate([chunks[k], swap(chunks[k], "seq", 1)], axis=0)
        grad_weight = grad_weight + mm(both, pair_all[k], TN)
    grad_weight = grad_weight.astype(BF16)

    partial = mm(attended, out_weight).astype(BF16).reshape(tensor_count, slab, model_width)
    mixed = partial[0].astype(F32)
    for bit in range(1, tensor_count):
        mixed = mixed + swap(partial[bit], "tensor", bit).astype(F32)
    layer_out = mixed.astype(BF16)[:piece].reshape(frames, tile_rows, local_columns, model_width)

    grad_attn = mm(g_all, out_weight, NT).astype(BF16)
    half = jax.ShapeDtypeStruct((2, tokens, channels), BF16)
    grad_q, grad_own, grad_above, grad_below = pl.pallas_call(
        backward_kernel,
        grid=(heads,),
        in_specs=list(common) + [row_spec, stat_spec],
        out_specs=[q_spec, kv_spec, kv_spec, kv_spec],
        out_shape=[
            jax.ShapeDtypeStruct((tokens, channels), BF16),
            jax.ShapeDtypeStruct((2, tokens, channels), F32),
            half,
            half,
        ],
        compiler_params=params,
        cost_estimate=pl.CostEstimate(flops=12 * work, bytes_accessed=18 * size, transcendentals=heads * rows * tokens * 3),
        name="backward",
    )(q_flat, kv_flat, kv_above, kv_below, row_bias, place, onehot, grad_attn, stats)
    from_below = shift(grad_above, "seq", -1).astype(F32)
    from_above = shift(grad_below, "seq", 1).astype(F32)
    grad_kv = (grad_own + from_below + from_above).astype(BF16).reshape(keys_values.shape)
    return (layer_out, grad_q.reshape(queries.shape), grad_kv, grad_weight)


def solution(mesh):
    return jax.shard_map(
        shards,
        mesh=mesh,
        in_specs=(
            P(None, "seq", None, "tensor"),
            P(None, None, "seq", None, "tensor"),
            P("tensor", None),
            P(None, "seq", "tensor", None),
            P("tensor", None),
            P(),
        ),
        out_specs=(
            P(None, "seq", "tensor", None),
            P(None, "seq", None, "tensor"),
            P(None, None, "seq", None, "tensor"),
            P("tensor", "seq"),
        ),
        check_vma=False,
    )
```

profile of v0, /device:TPU:1, one launch (start us, length us, event | category | flops | bytes accessed | tf_op | source)
XLA Modules:
  0.0 216.9 jit_solution(6370170515539019210)
XLA Ops:
  3.7 3.0 %collective-permute-start.7 = (bf16[96,5120]{1,0:T(8,128)(2,1)}, bf16[96,5120]{1,0:T(8,128)(2,1)S(1)}, u32[]{:S(2)}, u32[]{:S(2)}) collective-permute-start(bf16[96,5120]{1,0:T(8,128)(2,1)} %pad.9), channel_id=1, source_target_pairs={{0,3},{1,2},{2,1},{3,0},{4,7},{5,6},{6,5},{7,4},{8,11},{9,10},{10,... | collective-permute-start | bytes 2949128 | tf_op jit(solution)/shard_map/ppermute | solution.py:32
  7.0 3.4 %collective-permute-start.13 = (bf16[96,1280]{1,0:T(8,128)(2,1)S(1)}, bf16[96,1280]{1,0:T(8,128)(2,1)S(1)}, u32[]{:S(2)}, u32[]{:S(2)}) collective-permute-start(bf16[96,1280]{1,0:T(8,128)(2,1)S(1)} %get-tuple-element.43), channel_id=1, source_target_pairs={{0,24},{4,28},{8,0},{12,4},{16,8},{20,12},{24,16},{28,20},{1,25},{... | collective-permute-start | bytes 737288 | tf_op jit(solution)/shard_map/ppermute | solution.py:43
  11.6 2.9 %collective-permute-done.13 = bf16[96,1280]{1,0:T(8,128)(2,1)S(1)} collective-permute-done((bf16[96,1280]{1,0:T(8,128)(2,1)S(1)}, bf16[96,1280]{1,0:T(8,128)(2,1)S(1)}, u32[]{:S(2)}, u32[]{:S(2)}) %collective-permute-start.13) | collective-permute-done | bytes 245792 | tf_op jit(solution)/shard_map/ppermute | solution.py:43
  14.8 15.3 %collective-permute-done.12 = bf16[96,1280]{1,0:T(8,128)(2,1)S(1)} collective-permute-done((bf16[96,1280]{1,0:T(8,128)(2,1)S(1)}, bf16[96,1280]{1,0:T(8,128)(2,1)S(1)}, u32[]{:S(2)}, u32[]{:S(2)}) %collective-permute-start.12) | collective-permute-done | bytes 245792 | tf_op jit(solution)/shard_map/ppermute | solution.py:43
  32.3 2.8 %collective-permute-start.14 = (bf16[4,96,640]{2,1,0:T(8,128)(2,1)S(1)}, bf16[4,96,640]{2,1,0:T(8,128)(2,1)S(1)}, u32[]{:S(2)}, u32[]{:S(2)}) collective-permute-start(bf16[4,96,640]{2,1,0:T(8,128)(2,1)S(1)} %get-tuple-element.39), channel_id=1, source_target_pairs={{0,4},{4,0},{8,12},{12,8},{16,20},{20,16},{24,28},{28,24},{1,5},{5... | collective-permute-start | bytes 1474568 | tf_op jit(solution)/shard_map/ppermute | solution.py:32
  35.5 2.0 collective-permute-done.14
  43.7 7.3 %collective-permute-done.6 = bf16[96,5120]{1,0:T(8,128)(2,1)} collective-permute-done((bf16[96,5120]{1,0:T(8,128)(2,1)}, bf16[96,5120]{1,0:T(8,128)(2,1)}, u32[]{:S(2)}, u32[]{:S(2)}) %collective-permute-start.6) | collective-permute-done | bytes 983072 | tf_op jit(solution)/shard_map/ppermute | solution.py:32
  52.8 12.1 %fusion.11.g_ref = bf16[384,1280]{1,0:T(8,128)(2,1)} fusion(bf16[1280,5120]{1,0:T(8,128)(2,1)} %param.8, bf16[96,5120]{1,0:T(8,128)(2,1)} %copy-done.15, bf16[96,5120]{1,0:T(8,128)(2,1)} %collective-permute-done.6, bf16[96,5120]{1,0:T(8,128)(2,1)} %collective-permute-done.5, bf16[96,5120]{1,0:T(8,128)(2,1)} %pad.9), kind=kOutput, calls=%fused_computation.15 | convolution fusion | flops 5049384960 | bytes 18022400 | tf_op jit(solution)/shard_map/dot_general | solution.py:27
  64.9 15.4 %forward.1 = (bf16[384,1280]{1,0:T(8,128)(2,1)S(1)}, f32[10,8,384]{2,1,0:T(8,128)S(1)}) custom-call(bf16[360,1280]{1,0:T(8,128)(2,1)S(1)} %bitcast.48, bf16[2,360,1280]{2,1,0:T(8,128)(2,1)} %bitcast.1.own_ref, bf16[2,360,1280]{2,1,0:T(8,128)(2,1)} %collective-permute-done.above_ref, bf16[2,360,1280]{2,1,0:T(8,128)(2,1)} %collective-permute-done.1.below_ref, ...), custom_call_target="tpu_custom_call" | custom-call | flops 4246732800 | bytes 8294400 | tf_op jit(solution)/shard_map/forward/pallas_call | solution.py:202
  80.4 10.5 %convolution_convert_fusion = bf16[384,5120]{1,0:T(8,128)(2,1)S(1)} fusion(bf16[384,1280]{1,0:T(8,128)(2,1)S(1)} %get-tuple-element.10, bf16[1280,5120]{1,0:T(8,128)(2,1)} %param.8), kind=kOutput, calls=%fused_computation | convolution fusion | flops 5035130880 | bytes 18022400 | tf_op jit(solution)/shard_map/dot_general | solution.py:27
  90.8 3.9 %collective-permute-start.18 = (bf16[384,1280]{1,0:T(8,128)(2,1)S(1)}, bf16[384,1280]{1,0:T(8,128)(2,1)S(1)}, u32[]{:S(2)}, u32[]{:S(2)}) collective-permute-start(bf16[384,1280]{1,0:T(8,128)(2,1)S(1)} %get-tuple-element.10), channel_id=1, source_target_pairs={{0,8},{4,12},{8,16},{12,20},{16,24},{20,28},{1,9},{5,13},{9,17},{1... | collective-permute-start | bytes 2949128 | tf_op jit(solution)/shard_map/ppermute | solution.py:38
  97.5 2.4 %collective-permute-start.4 = (bf16[96,5120]{1,0:T(8,128)(2,1)}, bf16[96,5120]{1,0:T(8,128)(2,1)S(1)}, u32[]{:S(2)}, u32[]{:S(2)}) collective-permute-start(bf16[96,5120]{1,0:T(8,128)(2,1)} %get-tuple-element.33), channel_id=1, source_target_pairs={{0,3},{1,2},{2,1},{3,0},{4,7},{5,6},{6,5},{7,4},{8,11},{9,10},{10,... | collective-permute-start | bytes 2949128 | tf_op jit(solution)/shard_map/ppermute | solution.py:32
  100.2 14.7 %collective-permute-done.18 = bf16[384,1280]{1,0:T(8,128)(2,1)S(1)} collective-permute-done((bf16[384,1280]{1,0:T(8,128)(2,1)S(1)}, bf16[384,1280]{1,0:T(8,128)(2,1)S(1)}, u32[]{:S(2)}, u32[]{:S(2)}) %collective-permute-start.18) | collective-permute-done | bytes 983072 | tf_op jit(solution)/shard_map/ppermute | solution.py:38
  114.9 5.1 %collective-permute-start.23 = (bf16[384,1280]{1,0:T(8,128)(2,1)S(1)}, bf16[384,1280]{1,0:T(8,128)(2,1)}, u32[]{:S(2)}, u32[]{:S(2)}) collective-permute-start(bf16[384,1280]{1,0:T(8,128)(2,1)S(1)} %collective-permute-done.18), channel_id=1, source_target_pairs={{0,8},{4,12},{8,16},{12,20},{16,24},{20,28},{1,9},{5,13},{9,17},{1... | collective-permute-start | bytes 2949128 | tf_op jit(solution)/shard_map/ppermute | solution.py:38
  121.3 27.3 %backward.1 = (bf16[360,1280]{1,0:T(8,128)(2,1)}, f32[2,360,1280]{2,1,0:T(8,128)}, bf16[2,360,1280]{2,1,0:T(8,128)(2,1)}, bf16[2,360,1280]{2,1,0:T(8,128)(2,1)}) custom-call(bf16[360,1280]{1,0:T(8,128)(2,1)S(1)} %bitcast.49, bf16[2,360,1280]{2,1,0:T(8,128)(2,1)} %bitcast.1.own_ref, bf16[2,360,1280]{2,1,0:T(8,128)(2,1)} %collective-permute-done.above_ref, ...), custom_call_target="tpu_custom_call" | custom-call | flops 12740198400 | bytes 16588800 | tf_op jit(solution)/shard_map/backward/pallas_call | solution.py:235
  148.6 6.2 %collective-permute-start.9 = (bf16[2,360,1280]{2,1,0:T(8,128)(2,1)}, bf16[2,360,1280]{2,1,0:T(8,128)(2,1)}, u32[]{:S(2)}, u32[]{:S(2)}) collective-permute-start(bf16[2,360,1280]{2,1,0:T(8,128)(2,1)} %get-tuple-element.15), channel_id=1, source_target_pairs={{0,4},{4,8},{8,12},{12,16},{16,20},{20,24},{24,28},{1,5},{5,9},{9,... | collective-permute-start | bytes 5529608 | tf_op jit(solution)/shard_map/ppermute | solution.py:38
  156.8 2.1 pad_maximum_fusion
  163.7 2.7 %add.372 = bf16[384,1280]{1,0:T(8,128)(2,1)} add(bf16[384,1280]{1,0:T(8,128)(2,1)} %collective-permute-done.23, bf16[384,1280]{1,0:T(8,128)(2,1)} %collective-permute-done.20) | non-fusion elementwise | flops 491520 | bytes 2949120 | tf_op jit(solution)/shard_map/add | solution.py:220
  166.4 4.7 %collective-permute-start.25 = (bf16[384,1280]{1,0:T(8,128)(2,1)}, bf16[384,1280]{1,0:T(8,128)(2,1)}, u32[]{:S(2)}, u32[]{:S(2)}) collective-permute-start(bf16[384,1280]{1,0:T(8,128)(2,1)} %collective-permute-done.23), channel_id=1, source_target_pairs={{0,8},{4,12},{8,16},{12,20},{16,24},{20,28},{1,9},{5,13},{9,17},{1... | collective-permute-start | bytes 2949128 | tf_op jit(solution)/shard_map/ppermute | solution.py:38
  175.2 21.3 %collective-permute-done.25 = bf16[384,1280]{1,0:T(8,128)(2,1)} collective-permute-done((bf16[384,1280]{1,0:T(8,128)(2,1)}, bf16[384,1280]{1,0:T(8,128)(2,1)}, u32[]{:S(2)}, u32[]{:S(2)}) %collective-permute-start.25) | collective-permute-done | bytes 983072 | tf_op jit(solution)/shard_map/ppermute | solution.py:38
  197.9 3.7 %collective-permute-start.26 = (bf16[384,1280]{1,0:T(8,128)(2,1)S(1)}, bf16[384,1280]{1,0:T(8,128)(2,1)S(1)}, u32[]{:S(2)}, u32[]{:S(2)}) collective-permute-start(bf16[384,1280]{1,0:T(8,128)(2,1)S(1)} %add.374), channel_id=1, source_target_pairs={{0,4},{4,0},{8,12},{12,8},{16,20},{20,16},{24,28},{28,24},{1,5},{5... | collective-permute-start | bytes 2949128 | tf_op jit(solution)/shard_map/ppermute | solution.py:32
  203.1 3.9 %add_convert_fusion = bf16[2,360,1280]{2,1,0:T(8,128)(2,1)} fusion(bf16[2,360,1280]{2,1,0:T(8,128)(2,1)} %collective-permute-done.9, f32[2,360,1280]{2,1,0:T(8,128)S(1)} %copy-done.6, bf16[2,360,1280]{2,1,0:T(8,128)(2,1)} %collective-permute-done.8), kind=kLoop, calls=%fused_computation.10 | loop fusion | flops 4608000 | bytes 9216000 | tf_op jit(solution)/shard_map/convert_element_type | solution.py:252
  207.1 3.3 %fusion.21 = f32[1280,640]{1,0:T(8,128)S(1)} fusion(bf16[768,640]{1,0:T(8,128)(2,1)S(1)} %bitcast.54, bf16[384,1280]{1,0:T(8,128)(2,1)} %collective-permute-done.24, bf16[384,1280]{1,0:T(8,128)(2,1)} %add.372), kind=kOutput, calls=%fused_computation.23 | convolution fusion | flops 1262223360 | bytes 6225920 | tf_op jit(solution)/shard_map/dot_general | solution.py:27
  214.0 2.9 %fusion.10 = bf16[1280,640]{1,0:T(8,128)(2,1)} fusion(f32[1280,640]{1,0:T(8,128)S(1)} %fusion.25, f32[1280,640]{1,0:T(8,128)S(1)} %fusion.21, f32[1280,640]{1,0:T(8,128)S(1)} %fusion.17, bf16[768,640]{1,0:T(8,128)(2,1)S(1)} %bitcast.50, bf16[384,1280]{1,0:T(8,128)(2,1)S(1)} %collective-permute-done.10, bf16[384,1280]{1,0:T(8,128)(2,1)S(1)} %get-tuple-element.10), kind=kOutput, calls=%fused_computation.14 | convolution fusion | flops 1265500160 | bytes 14417920 | tf_op jit(solution)/shard_map/dot_general | solution.py:27
  (114 shorter events, 36.8 us)
Async XLA Ops:
  3.7 37.9 %collective-permute-start.7 = (bf16[96,5120]{1,0:T(8,128)(2,1)}, bf16[96,5120]{1,0:T(8,128)(2,1)S(1)}, u32[]{:S(2)}, u32[]{:S(2)}) collective-permute-start(bf16[96,5120]{1,0:T(8,128)(2,1)} %pad.9), channel_id=1, source_target_pairs={{0,3},{1,2},{2,1},{3,0},{4,7},{5,6},{6,5},{7,4},{8,11},{9,10},{10,... | collective-permute-start | bytes 2949128 | tf_op jit(solution)/shard_map/ppermute | solution.py:32
  6.7 44.3 %collective-permute-start.6 = (bf16[96,5120]{1,0:T(8,128)(2,1)}, bf16[96,5120]{1,0:T(8,128)(2,1)}, u32[]{:S(2)}, u32[]{:S(2)}) collective-permute-start(bf16[96,5120]{1,0:T(8,128)(2,1)} %pad.9), channel_id=1, source_target_pairs={{0,2},{1,3},{2,0},{3,1},{4,6},{5,7},{6,4},{7,5},{8,10},{9,11},{10,... | collective-permute-start | bytes 2949128 | tf_op jit(solution)/shard_map/ppermute | solution.py:32
  10.4 19.7 %collective-permute-start.12 = (bf16[96,1280]{1,0:T(8,128)(2,1)S(1)}, bf16[96,1280]{1,0:T(8,128)(2,1)S(1)}, u32[]{:S(2)}, u32[]{:S(2)}) collective-permute-start(bf16[96,1280]{1,0:T(8,128)(2,1)S(1)} %get-tuple-element.42), channel_id=1, source_target_pairs={{0,16},{4,20},{8,24},{12,28},{16,0},{20,4},{24,8},{28,12},{1,17},{... | collective-permute-start | bytes 737288 | tf_op jit(solution)/shard_map/ppermute | solution.py:43
  10.4 21.6 %collective-permute-start.11 = (bf16[96,1280]{1,0:T(8,128)(2,1)S(1)}, bf16[96,1280]{1,0:T(8,128)(2,1)S(1)}, u32[]{:S(2)}, u32[]{:S(2)}) collective-permute-start(bf16[96,1280]{1,0:T(8,128)(2,1)S(1)} %get-tuple-element.41), channel_id=1, source_target_pairs={{0,8},{4,12},{8,16},{12,20},{16,24},{20,28},{24,0},{28,4},{1,9},{5... | collective-permute-start | bytes 737288 | tf_op jit(solution)/shard_map/ppermute | solution.py:43
  14.6 38.2 %collective-permute-start.5 = (bf16[96,5120]{1,0:T(8,128)(2,1)}, bf16[96,5120]{1,0:T(8,128)(2,1)}, u32[]{:S(2)}, u32[]{:S(2)}) collective-permute-start(bf16[96,5120]{1,0:T(8,128)(2,1)} %pad.9), channel_id=1, source_target_pairs={{0,1},{1,0},{2,3},{3,2},{4,5},{5,4},{6,7},{7,6},{8,9},{9,8},{10,11... | collective-permute-start | bytes 2949128 | tf_op jit(solution)/shard_map/ppermute | solution.py:32
  30.1 34.8 %collective-permute-start = (bf16[2,360,1280]{2,1,0:T(8,128)(2,1)}, bf16[2,360,1280]{2,1,0:T(8,128)(2,1)}, u32[]{:S(2)}, u32[]{:S(2)}) collective-permute-start(bf16[2,360,1280]{2,1,0:T(8,128)(2,1)} %bitcast.1.own_ref), channel_id=1, source_target_pairs={{0,4},{4,8},{8,12},{12,16},{16,20},{20,24},{24,28},{1,5},{5,9},{9,... | collective-permute-start | bytes 5529608 | tf_op jit(solution)/shard_map/ppermute | solution.py:38
  37.5 27.4 %collective-permute-start.1 = (bf16[2,360,1280]{2,1,0:T(8,128)(2,1)}, bf16[2,360,1280]{2,1,0:T(8,128)(2,1)}, u32[]{:S(2)}, u32[]{:S(2)}) collective-permute-start(bf16[2,360,1280]{2,1,0:T(8,128)(2,1)} %bitcast.1.own_ref), channel_id=1, source_target_pairs={{4,0},{8,4},{12,8},{16,12},{20,16},{24,20},{28,24},{5,1},{9,5},{13... | collective-permute-start | bytes 5529608 | tf_op jit(solution)/shard_map/ppermute | solution.py:38
  42.5 54.9 %collective-permute-start.17 = (bf16[4,2,96,640]{3,2,0,1:T(8,128)(2,1)}, bf16[4,2,96,640]{3,2,0,1:T(8,128)(2,1)}, u32[]{:S(2)}, u32[]{:S(2)}) collective-permute-start(bf16[4,2,96,640]{3,2,0,1:T(8,128)(2,1)} %get-tuple-element.37), channel_id=1, source_target_pairs={{0,3},{1,2},{2,1},{3,0},{4,7},{5,6},{6,5},{7,4},{8,11},{9,10},{10,... | collective-permute-start | bytes 2949128 | tf_op jit(solution)/shard_map/ppermute | solution.py:32
  51.0 48.9 %collective-permute-start.16 = (bf16[4,2,96,640]{3,2,0,1:T(8,128)(2,1)}, bf16[4,2,96,640]{3,2,0,1:T(8,128)(2,1)}, u32[]{:S(2)}, u32[]{:S(2)}) collective-permute-start(bf16[4,2,96,640]{3,2,0,1:T(8,128)(2,1)} %get-tuple-element.37), channel_id=1, source_target_pairs={{0,2},{1,3},{2,0},{3,1},{4,6},{5,7},{6,4},{7,5},{8,10},{9,11},{10,... | collective-permute-start | bytes 2949128 | tf_op jit(solution)/shard_map/ppermute | solution.py:32
  52.8 47.3 %collective-permute-start.15 = (bf16[4,2,96,640]{3,2,0,1:T(8,128)(2,1)}, bf16[4,2,96,640]{3,2,0,1:T(8,128)(2,1)}, u32[]{:S(2)}, u32[]{:S(2)}) collective-permute-start(bf16[4,2,96,640]{3,2,0,1:T(8,128)(2,1)} %get-tuple-element.37), channel_id=1, source_target_pairs={{0,1},{1,0},{2,3},{3,2},{4,5},{5,4},{6,7},{7,6},{8,9},{9,8},{10,11... | collective-permute-start | bytes 2949128 | tf_op jit(solution)/shard_map/ppermute | solution.py:32
  90.8 24.1 %collective-permute-start.18 = (bf16[384,1280]{1,0:T(8,128)(2,1)S(1)}, bf16[384,1280]{1,0:T(8,128)(2,1)S(1)}, u32[]{:S(2)}, u32[]{:S(2)}) collective-permute-start(bf16[384,1280]{1,0:T(8,128)(2,1)S(1)} %get-tuple-element.10), channel_id=1, source_target_pairs={{0,8},{4,12},{8,16},{12,20},{16,24},{20,28},{1,9},{5,13},{9,17},{1... | collective-permute-start | bytes 2949128 | tf_op jit(solution)/shard_map/ppermute | solution.py:38
  94.8 25.2 %collective-permute-start.19 = (bf16[384,1280]{1,0:T(8,128)(2,1)S(1)}, bf16[384,1280]{1,0:T(8,128)(2,1)S(1)}, u32[]{:S(2)}, u32[]{:S(2)}) collective-permute-start(bf16[384,1280]{1,0:T(8,128)(2,1)S(1)} %get-tuple-element.10), channel_id=1, source_target_pairs={{8,0},{12,4},{16,8},{20,12},{24,16},{28,20},{9,1},{13,5},{17,9},{2... | collective-permute-start | bytes 2949128 | tf_op jit(solution)/shard_map/ppermute | solution.py:38
  97.5 68.9 %collective-permute-start.4 = (bf16[96,5120]{1,0:T(8,128)(2,1)}, bf16[96,5120]{1,0:T(8,128)(2,1)S(1)}, u32[]{:S(2)}, u32[]{:S(2)}) collective-permute-start(bf16[96,5120]{1,0:T(8,128)(2,1)} %get-tuple-element.33), channel_id=1, source_target_pairs={{0,3},{1,2},{2,1},{3,0},{4,7},{5,6},{6,5},{7,4},{8,11},{9,10},{10,... | collective-permute-start | bytes 2949128 | tf_op jit(solution)/shard_map/ppermute | solution.py:32
  99.9 66.5 %collective-permute-start.3 = (bf16[96,5120]{1,0:T(8,128)(2,1)S(1)}, bf16[96,5120]{1,0:T(8,128)(2,1)S(1)}, u32[]{:S(2)}, u32[]{:S(2)}) collective-permute-start(bf16[96,5120]{1,0:T(8,128)(2,1)S(1)} %get-tuple-element.34), channel_id=1, source_target_pairs={{0,2},{1,3},{2,0},{3,1},{4,6},{5,7},{6,4},{7,5},{8,10},{9,11},{10,... | collective-permute-start | bytes 2949128 | tf_op jit(solution)/shard_map/ppermute | solution.py:32
  100.1 71.0 %collective-permute-start.2 = (bf16[96,5120]{1,0:T(8,128)(2,1)S(1)}, bf16[96,5120]{1,0:T(8,128)(2,1)S(1)}, u32[]{:S(2)}, u32[]{:S(2)}) collective-permute-start(bf16[96,5120]{1,0:T(8,128)(2,1)S(1)} %get-tuple-element.35), channel_id=1, source_target_pairs={{0,1},{1,0},{2,3},{3,2},{4,5},{5,4},{6,7},{7,6},{8,9},{9,8},{10,11... | collective-permute-start | bytes 2949128 | tf_op jit(solution)/shard_map/ppermute | solution.py:32
  114.9 33.7 %collective-permute-start.23 = (bf16[384,1280]{1,0:T(8,128)(2,1)S(1)}, bf16[384,1280]{1,0:T(8,128)(2,1)}, u32[]{:S(2)}, u32[]{:S(2)}) collective-permute-start(bf16[384,1280]{1,0:T(8,128)(2,1)S(1)} %collective-permute-done.18), channel_id=1, source_target_pairs={{0,8},{4,12},{8,16},{12,20},{16,24},{20,28},{1,9},{5,13},{9,17},{1... | collective-permute-start | bytes 2949128 | tf_op jit(solution)/shard_map/ppermute | solution.py:38
  120.0 34.9 %collective-permute-start.20 = (bf16[384,1280]{1,0:T(8,128)(2,1)S(1)}, bf16[384,1280]{1,0:T(8,128)(2,1)}, u32[]{:S(2)}, u32[]{:S(2)}) collective-permute-start(bf16[384,1280]{1,0:T(8,128)(2,1)S(1)} %collective-permute-done.19), channel_id=1, source_target_pairs={{8,0},{12,4},{16,8},{20,12},{24,16},{28,20},{9,1},{13,5},{17,9},{2... | collective-permute-start | bytes 2949128 | tf_op jit(solution)/shard_map/ppermute | solution.py:38
  148.6 54.4 %collective-permute-start.9 = (bf16[2,360,1280]{2,1,0:T(8,128)(2,1)}, bf16[2,360,1280]{2,1,0:T(8,128)(2,1)}, u32[]{:S(2)}, u32[]{:S(2)}) collective-permute-start(bf16[2,360,1280]{2,1,0:T(8,128)(2,1)} %get-tuple-element.15), channel_id=1, source_target_pairs={{0,4},{4,8},{8,12},{12,16},{16,20},{20,24},{24,28},{1,5},{5,9},{9,... | collective-permute-start | bytes 5529608 | tf_op jit(solution)/shard_map/ppermute | solution.py:38
  154.9 48.2 %collective-permute-start.8 = (bf16[2,360,1280]{2,1,0:T(8,128)(2,1)}, bf16[2,360,1280]{2,1,0:T(8,128)(2,1)}, u32[]{:S(2)}, u32[]{:S(2)}) collective-permute-start(bf16[2,360,1280]{2,1,0:T(8,128)(2,1)} %get-tuple-element.14), channel_id=1, source_target_pairs={{4,0},{8,4},{12,8},{16,12},{20,16},{24,20},{28,24},{5,1},{9,5},{13... | collective-permute-start | bytes 5529608 | tf_op jit(solution)/shard_map/ppermute | solution.py:38
  166.4 40.7 %collective-permute-start.24 = (bf16[384,1280]{1,0:T(8,128)(2,1)}, bf16[384,1280]{1,0:T(8,128)(2,1)}, u32[]{:S(2)}, u32[]{:S(2)}) collective-permute-start(bf16[384,1280]{1,0:T(8,128)(2,1)} %add.372), channel_id=1, source_target_pairs={{0,4},{4,0},{8,12},{12,8},{16,20},{20,16},{24,28},{28,24},{1,5},{5... | collective-permute-start | bytes 2949128 | tf_op jit(solution)/shard_map/ppermute | solution.py:32
  166.4 30.1 %collective-permute-start.25 = (bf16[384,1280]{1,0:T(8,128)(2,1)}, bf16[384,1280]{1,0:T(8,128)(2,1)}, u32[]{:S(2)}, u32[]{:S(2)}) collective-permute-start(bf16[384,1280]{1,0:T(8,128)(2,1)} %collective-permute-done.23), channel_id=1, source_target_pairs={{0,8},{4,12},{8,16},{12,20},{16,24},{20,28},{1,9},{5,13},{9,17},{1... | collective-permute-start | bytes 2949128 | tf_op jit(solution)/shard_map/ppermute | solution.py:38
  171.1 26.8 %collective-permute-start.21 = (bf16[384,1280]{1,0:T(8,128)(2,1)}, bf16[384,1280]{1,0:T(8,128)(2,1)}, u32[]{:S(2)}, u32[]{:S(2)}) collective-permute-start(bf16[384,1280]{1,0:T(8,128)(2,1)} %collective-permute-done.20), channel_id=1, source_target_pairs={{8,0},{12,4},{16,8},{20,12},{24,16},{28,20},{9,1},{13,5},{17,9},{2... | collective-permute-start | bytes 2949128 | tf_op jit(solution)/shard_map/ppermute | solution.py:38
  196.5 17.5 %collective-permute-start.10 = (bf16[384,1280]{1,0:T(8,128)(2,1)S(1)}, bf16[384,1280]{1,0:T(8,128)(2,1)S(1)}, u32[]{:S(2)}, u32[]{:S(2)}) collective-permute-start(bf16[384,1280]{1,0:T(8,128)(2,1)S(1)} %get-tuple-element.10), channel_id=1, source_target_pairs={{0,4},{4,0},{8,12},{12,8},{16,20},{20,16},{24,28},{28,24},{1,5},{5... | collective-permute-start | bytes 2949128 | tf_op jit(solution)/shard_map/ppermute | solution.py:32
  197.9 12.5 %collective-permute-start.26 = (bf16[384,1280]{1,0:T(8,128)(2,1)S(1)}, bf16[384,1280]{1,0:T(8,128)(2,1)S(1)}, u32[]{:S(2)}, u32[]{:S(2)}) collective-permute-start(bf16[384,1280]{1,0:T(8,128)(2,1)S(1)} %add.374), channel_id=1, source_target_pairs={{0,4},{4,0},{8,12},{12,8},{16,20},{20,16},{24,28},{28,24},{1,5},{5... | collective-permute-start | bytes 2949128 | tf_op jit(solution)/shard_map/ppermute | solution.py:32
  (19 other events, 285.4 us)
where the time goes:
time: 218 us; the launch traced here: 217 us
  waiting for transfers between devices  63.5 us (29%)
  starting transfers between devices  49.4 us (23%)
  Pallas kernels  42.7 us (20%)
  matrix products  32.3 us (15%)
  other arithmetic  15.2 us (7%)
  local copies, waits for them, and re-layouts  12.5 us (6%)
    ppermute x10, waiting for transfers between devices, shift(): return lax.ppermute(value, axis, pairs)  35.9 us
    dot_general x6, matrix products, mm(): return lax.dot_general(left, right, dims, preferred_element_type=F32)  32.3 us
    ppermute x10, starting transfers between devices, shift(): return lax.ppermute(value, axis, pairs)  29.8 us
    pallas_call x1, Pallas kernels, shards(): pl.pallas_call(backward_kernel, grid=(heads,), in_specs=list(common) + [r...  27.3 us
    ppermute x3, waiting for transfers between devices, turn(): lax.ppermute(value, axis, [(i, (i + steps) % count) for i in range(count)])  18.2 us
    ppermute x14, starting transfers between devices, swap(): return lax.ppermute(value, axis, [(i, i ^ bit) for i in range(count)])  15.7 us
    pallas_call x1, Pallas kernels, shards(): pl.pallas_call(forward_kernel, grid=(heads,), in_specs=list(common), out_...  15.4 us
    ppermute x14, waiting for transfers between devices, swap(): return lax.ppermute(value, axis, [(i, i ^ bit) for i in range(count)])  9.32 us
  transfers between devices with their start and end apart: 27, of which 6 were waited for; matrix products, arithmetic and copies ran while one was open for 24% of the time, Pallas kernels for 20%

commit v1 on v0

--- a/solution.py
+++ b/solution.py
@@ -146,12 +146,12 @@
     kv_below = shift(kv_flat, "seq", -1)
 
     g_own = jnp.pad(grad_out.reshape(piece, model_width), ((0, slab - piece), (0, 0)))
-    g_all = jnp.concatenate(
-        [g_own] + [swap(g_own, "tensor", bit) for bit in range(1, tensor_count)], axis=0
-    )
+    g_pieces = [g_own] + [swap(g_own, "tensor", bit) for bit in range(1, tensor_count)]
+
+    g_later, kv_above, kv_below = lax.optimization_barrier((g_own, kv_above, kv_below))
 
     def columns_for(place):
-        return lax.dynamic_slice_in_dim(g_own, place * 2 * width, 2 * width, axis=1)
+        return lax.dynamic_slice_in_dim(g_later, place * 2 * width, 2 * width, axis=1)
 
     moved = jnp.stack(
         [columns_for(chip)]
@@ -215,8 +215,9 @@
 
     ups, downs = [attended], [attended]
     for _ in range(1, chips):
-        ups.append(shift(ups[-1], "seq", 2))
-        downs.append(shift(downs[-1], "seq", -2))
+        up, down = lax.optimization_barrier((ups[-1], downs[-1]))
+        ups.append(shift(up, "seq", 2))
+        downs.append(shift(down, "seq", -2))
     chunks = [attended] + [ups[k] + downs[chips - k] for k in range(1, chips)]
     grad_weight = jnp.zeros((channels, width), F32)
     for k in range(chips):
@@ -224,29 +225,58 @@
         grad_weight = grad_weight + mm(both, pair_all[k], TN)
     grad_weight = grad_weight.astype(BF16)
 
+    first, last = min(1, chips - 1), min(2, chips - 1)
+    *g_pieces, _ = lax.optimization_barrier((*g_pieces, attended))
+    grad_attn = mm(jnp.concatenate(g_pieces, axis=0), out_weight, NT).astype(BF16)
+    attended, _, _ = lax.optimization_barrier((attended, ups[first], downs[first]))
     partial = mm(attended, out_weight).astype(BF16).reshape(tensor_count, slab, model_width)
     mixed = partial[0].astype(F32)
     for bit in range(1, tensor_count):
         mixed = mixed + swap(partial[bit], "tensor", bit).astype(F32)
     layer_out = mixed.astype(BF16)[:piece].reshape(frames, tile_rows, local_columns, model_width)
 
-    grad_attn = mm(g_all, out_weight, NT).astype(BF16)
     half = jax.ShapeDtypeStruct((2, tokens, channels), BF16)
-    grad_q, grad_own, grad_above, grad_below = pl.pallas_call(
-        backward_kernel,
-        grid=(heads,),
-        in_specs=list(common) + [row_spec, stat_spec],
-        out_specs=[q_spec, kv_spec, kv_spec, kv_spec],
-        out_shape=[
-            jax.ShapeDtypeStruct((tokens, channels), BF16),
-            jax.ShapeDtypeStruct((2, tokens, channels), F32),
-            half,
-            half,
-        ],
-        compiler_params=params,
-        cost_estimate=pl.CostEstimate(flops=12 * work, bytes_accessed=18 * size, transcendentals=heads * rows * tokens * 3),
-        name="backward",
-    )(q_flat, kv_flat, kv_above, kv_below, row_bias, place, onehot, grad_attn, stats)
+    grad_shapes = [
+        jax.ShapeDtypeStruct((tokens, channels), BF16),
+        jax.ShapeDtypeStruct((2, tokens, channels), F32),
+        half,
+        half,
+    ]
+
+    def backward(first_head, count, stats, grads):
+        def moved_spec(spec):
+            index_map = spec.index_map
+            return pl.BlockSpec(spec.block_shape, lambda h: index_map(h + first_head))
+
+        def body(*refs):
+            backward_kernel(*refs[:9], *refs[9 + len(grads) :])
+
+        specs = list(common) + [row_spec, stat_spec]
+        return pl.pallas_call(
+            body,
+            grid=(count,),
+            in_specs=[moved_spec(spec) for spec in specs]
+            + [pl.BlockSpec(memory_space=pl.ANY)] * len(grads),
+            out_specs=[moved_spec(spec) for spec in (q_spec, kv_spec, kv_spec, kv_spec)],
+            out_shape=grad_shapes,
+            input_output_aliases={9 + i: i for i in range(len(grads))},
+            compiler_params=params,
+            cost_estimate=pl.CostEstimate(
+                flops=12 * work * count // heads,
+                bytes_accessed=18 * size * count // heads,
+                transcendentals=count * rows * tokens * 3,
+            ),
+            name="backward",
+        )(q_flat, kv_flat, kv_above, kv_below, row_bias, place, onehot, grad_attn, stats, *grads)
+
+    cut = heads // 2
+    stats, _, _ = lax.optimization_barrier((stats, ups[first], downs[first]))
+    grads = backward(0, cut, stats, ())
+    stats, _, _ = lax.optimization_barrier((stats, ups[last], downs[last]))
+    grad_q, grad_own, grad_above, grad_below = backward(cut, heads - cut, stats, tuple(grads))
+    grad_above, grad_below, _, _ = lax.optimization_barrier(
+        (grad_above, grad_below, ups[-1], downs[-1])
+    )
     from_below = shift(grad_above, "seq", -1).astype(F32)
     from_above = shift(grad_below, "seq", 1).astype(F32)
     grad_kv = (grad_own + from_below + from_above).astype(BF16).reshape(keys_values.shape)

time: 218 us -> 199 us (0.913)
  waiting for transfers between devices: 63.5 us -> 34.1 us
  matrix products: 32.3 us -> 35.8 us
  local copies, waits for them, and re-layouts: 12.5 us -> 15.1 us
  other arithmetic: 15.2 us -> 17.7 us
    ppermute x3, waiting for transfers between devices: 18.2 us -> 0.01 us  [turn(): lax.ppermute(value, axis, [(i, (i + steps) % count) for i in range(count)])]
    ppermute x10, waiting for transfers between devices: 35.9 us -> 22.7 us  [shift(): return lax.ppermute(value, axis, pairs)]
    dot_general x6, matrix products: 32.3 us -> 35.8 us  [mm(): return lax.dot_general(left, right, dims, preferred_element_type=F32)]
    add x3, other arithmetic: 5.54 us -> 8.03 us  [shards(): chunks = [attended] + [ups[k] + downs[chips - k] for k in range(1, chips)]]
    pallas_call x1 -> x2, Pallas kernels: 27.3 us -> 28.9 us  [backward(): pl.pallas_call(body, grid=(count,), in_specs=[moved_spec(spec) for spec i...]
    unnamed x35 -> x25, local copies, waits for them, and re-layouts: 4.54 us -> 4.24 us
  transfers between devices with their start and end apart: 27 -> 27, of which waited for: 6 -> 6; matrix products, arithmetic and copies ran while one was open for 24% -> 31% of each run, Pallas kernels for 20% -> 22%
where the time goes in v1:
time: 199 us; the launch traced here: 198 us
  starting transfers between devices  50.2 us (25%)
  Pallas kernels  44.3 us (22%)
  matrix products  35.8 us (18%)
  waiting for transfers between devices  34.1 us (17%)
  other arithmetic  17.7 us (9%)
  local copies, waits for them, and re-layouts  15.1 us (8%)
    dot_general x6, matrix products, mm(): return lax.dot_general(left, right, dims, preferred_element_type=F32)  35.8 us
    ppermute x10, starting transfers between devices, shift(): return lax.ppermute(value, axis, pairs)  30.7 us
    pallas_call x2, Pallas kernels, backward(): pl.pallas_call(body, grid=(count,), in_specs=[moved_spec(spec) for spec i...  28.9 us
    ppermute x10, waiting for transfers between devices, shift(): return lax.ppermute(value, axis, pairs)  22.7 us
    ppermute x14, starting transfers between devices, swap(): return lax.ppermute(value, axis, [(i, i ^ bit) for i in range(count)])  15.7 us
    pallas_call x1, Pallas kernels, shards(): pl.pallas_call(forward_kernel, grid=(heads,), in_specs=list(common), out_...  15.4 us
    ppermute x14, waiting for transfers between devices, swap(): return lax.ppermute(value, axis, [(i, i ^ bit) for i in range(count)])  11.4 us
    add x3, other arithmetic, shards(): chunks = [attended] + [ups[k] + downs[chips - k] for k in range(1, chips)]  8.03 us
  transfers between devices with their start and end apart: 27, of which 6 were waited for; matrix products, arithmetic and copies ran while one was open for 31% of the time, Pallas kernels for 22%

profile of v1, /device:TPU:1, one launch (start us, length us, event | category | flops | bytes accessed | tf_op | source)
XLA Modules:
  0.0 198.4 jit_solution(10923117431346475941)
XLA Ops:
  3.7 3.0 %collective-permute-start.9 = (bf16[96,5120]{1,0:T(8,128)(2,1)}, bf16[96,5120]{1,0:T(8,128)(2,1)}, u32[]{:S(2)}, u32[]{:S(2)}) collective-permute-start(bf16[96,5120]{1,0:T(8,128)(2,1)} %pad.8), channel_id=1, source_target_pairs={{0,3},{1,2},{2,1},{3,0},{4,7},{5,6},{6,5},{7,4},{8,11},{9,10},{10,... | collective-permute-start | bytes 2949128 | tf_op jit(solution)/shard_map/ppermute | solution.py:32
  7.0 3.1 %collective-permute-start.1 = (bf16[2,360,1280]{2,1,0:T(8,128)(2,1)}, bf16[2,360,1280]{2,1,0:T(8,128)(2,1)}, u32[]{:S(2)}, u32[]{:S(2)}) collective-permute-start(bf16[2,360,1280]{2,1,0:T(8,128)(2,1)} %bitcast.1.own_ref.refs_1_), channel_id=1, source_target_pairs={{4,0},{8,4},{12,8},{16,12},{20,16},{24,20},{28,24},{5,1},{9,5},{13... | collective-permute-start | bytes 5529608 | tf_op jit(solution)/shard_map/ppermute | solution.py:38
  10.2 3.6 %collective-permute-start = (bf16[2,360,1280]{2,1,0:T(8,128)(2,1)}, bf16[2,360,1280]{2,1,0:T(8,128)(2,1)}, u32[]{:S(2)}, u32[]{:S(2)}) collective-permute-start(bf16[2,360,1280]{2,1,0:T(8,128)(2,1)} %bitcast.1.own_ref.refs_1_), channel_id=1, source_target_pairs={{0,4},{4,8},{8,12},{12,16},{16,20},{20,24},{24,28},{1,5},{5,9},{9,... | collective-permute-start | bytes 5529608 | tf_op jit(solution)/shard_map/ppermute | solution.py:38
  15.5 17.9 %collective-permute-done.1.below_ref.refs_3_ = bf16[2,360,1280]{2,1,0:T(8,128)(2,1)} collective-permute-done((bf16[2,360,1280]{2,1,0:T(8,128)(2,1)}, bf16[2,360,1280]{2,1,0:T(8,128)(2,1)}, u32[]{:S(2)}, u32[]{:S(2)}) %collective-permute-start.1) | collective-permute-done | bytes 1843232 | tf_op jit(solution)/shard_map/ppermute | solution.py:38
  39.5 15.4 %forward.1 = (bf16[384,1280]{1,0:T(8,128)(2,1)S(1)}, f32[10,8,384]{2,1,0:T(8,128)S(1)}) custom-call(bf16[360,1280]{1,0:T(8,128)(2,1)S(1)} %bitcast.48, bf16[2,360,1280]{2,1,0:T(8,128)(2,1)} %bitcast.1.own_ref.refs_1_, bf16[2,360,1280]{2,1,0:T(8,128)(2,1)} %collective-permute-done.above_ref.refs_2_, ...), custom_call_target="tpu_custom_call" | custom-call | flops 4246732800 | bytes 8294400 | tf_op jit(solution)/shard_map/forward/pallas_call | solution.py:202
  55.6 2.9 %collective-permute-start.2 = (bf16[384,1280]{1,0:T(8,128)(2,1)S(1)}, bf16[384,1280]{1,0:T(8,128)(2,1)}, u32[]{:S(2)}, u32[]{:S(2)}) collective-permute-start(bf16[384,1280]{1,0:T(8,128)(2,1)S(1)} %get-tuple-element.37), channel_id=1, source_target_pairs={{0,8},{4,12},{8,16},{12,20},{16,24},{20,28},{1,9},{5,13},{9,17},{1... | collective-permute-start | bytes 2949128 | tf_op jit(solution)/shard_map/ppermute | solution.py:38
  61.0 4.6 %collective-permute-start.20 = (bf16[4,96,640]{2,1,0:T(8,128)(2,1)}, bf16[4,96,640]{2,1,0:T(8,128)(2,1)}, u32[]{:S(2)}, u32[]{:S(2)}) collective-permute-start(bf16[4,96,640]{2,1,0:T(8,128)(2,1)} %get-tuple-element.83), channel_id=1, source_target_pairs={{0,4},{4,0},{8,12},{12,8},{16,20},{20,16},{24,28},{28,24},{1,5},{5... | collective-permute-start | bytes 1474568 | tf_op jit(solution)/shard_map/ppermute | solution.py:32
  65.6 12.1 %fusion.11.refs_7_ = bf16[384,1280]{1,0:T(8,128)(2,1)} fusion(bf16[1280,5120]{1,0:T(8,128)(2,1)} %param.8, bf16[96,5120]{1,0:T(8,128)(2,1)} %collective-permute-done.9, bf16[96,5120]{1,0:T(8,128)(2,1)} %collective-permute-done.8, bf16[96,5120]{1,0:T(8,128)(2,1)} %collective-permute-done.7, bf16[96,5120]{1,0:T(8,128)(2,1)} %pad.8), kind=kOutput, calls=%fused_computation.15 | convolution fusion | flops 5049384960 | bytes 18022400 | tf_op jit(solution)/shard_map/dot_general | solution.py:27
  81.8 5.4 %collective-permute-start.10 = (bf16[384,1280]{1,0:T(8,128)(2,1)}, bf16[384,1280]{1,0:T(8,128)(2,1)}, u32[]{:S(2)}, u32[]{:S(2)}) collective-permute-start(bf16[384,1280]{1,0:T(8,128)(2,1)} %collective-permute-done.2), channel_id=1, source_target_pairs={{0,8},{4,12},{8,16},{12,20},{16,24},{20,28},{1,9},{5,13},{9,17},{1... | collective-permute-start | bytes 2949128 | tf_op jit(solution)/shard_map/ppermute | solution.py:38
  88.7 10.2 %convolution_convert_fusion = bf16[384,5120]{1,0:T(8,128)(2,1)S(1)} fusion(bf16[384,1280]{1,0:T(8,128)(2,1)S(1)} %get-tuple-element.37, bf16[1280,5120]{1,0:T(8,128)(2,1)} %param.8), kind=kOutput, calls=%fused_computation | convolution fusion | flops 5035130880 | bytes 18022400 | tf_op jit(solution)/shard_map/dot_general | solution.py:27
  98.9 14.5 %backward.2 = (bf16[360,1280]{1,0:T(8,128)(2,1)}, f32[2,360,1280]{2,1,0:T(8,128)}, bf16[2,360,1280]{2,1,0:T(8,128)(2,1)}, bf16[2,360,1280]{2,1,0:T(8,128)(2,1)}) custom-call(bf16[360,1280]{1,0:T(8,128)(2,1)S(1)} %bitcast.49, bf16[2,360,1280]{2,1,0:T(8,128)(2,1)} %bitcast.1.own_ref.refs_1_, bf16[2,360,1280]{2,1,0:T(8,128)(2,1)} %collective-permute-done.above_ref.refs_2_, ...), custom_call_target="tpu_custom_call" | custom-call | flops 6370099200 | bytes 8294400 | tf_op jit(solution)/shard_map/backward/pallas_call | solution.py:255
  117.7 4.9 %collective-permute-start.12 = (bf16[384,1280]{1,0:T(8,128)(2,1)}, bf16[384,1280]{1,0:T(8,128)(2,1)}, u32[]{:S(2)}, u32[]{:S(2)}) collective-permute-start(bf16[384,1280]{1,0:T(8,128)(2,1)} %collective-permute-done.10), channel_id=1, source_target_pairs={{0,8},{4,12},{8,16},{12,20},{16,24},{20,28},{1,9},{5,13},{9,17},{1... | collective-permute-start | bytes 2949128 | tf_op jit(solution)/shard_map/ppermute | solution.py:38
  132.9 2.7 %add.380 = bf16[384,1280]{1,0:T(8,128)(2,1)} add(bf16[384,1280]{1,0:T(8,128)(2,1)} %collective-permute-done.10, bf16[384,1280]{1,0:T(8,128)(2,1)} %collective-permute-done.11) | non-fusion elementwise | flops 491520 | bytes 2949120 | tf_op jit(solution)/shard_map/add | solution.py:221
  135.6 14.4 %backward.3 = (bf16[360,1280]{1,0:T(8,128)(2,1)}, f32[2,360,1280]{2,1,0:T(8,128)}, bf16[2,360,1280]{2,1,0:T(8,128)(2,1)}, bf16[2,360,1280]{2,1,0:T(8,128)(2,1)}) custom-call(bf16[360,1280]{1,0:T(8,128)(2,1)S(1)} %bitcast.50, ...), custom_call_target="tpu_custom_call", output_to_operand_aliasing={{0}: (9, {}), {1}: (10, {}), {2}: (11, {}), {3}: (12, {})} | custom-call | flops 6370099200 | bytes 8294400 | tf_op jit(solution)/shard_map/backward/pallas_call | solution.py:255
  151.9 2.7 %add.382 = bf16[384,1280]{1,0:T(8,128)(2,1)} add(bf16[384,1280]{1,0:T(8,128)(2,1)} %collective-permute-done.12, bf16[384,1280]{1,0:T(8,128)(2,1)} %collective-permute-done.3) | non-fusion elementwise | flops 491520 | bytes 2949120 | tf_op jit(solution)/shard_map/add | solution.py:221
  154.7 2.7 %add.378 = bf16[384,1280]{1,0:T(8,128)(2,1)} add(bf16[384,1280]{1,0:T(8,128)(2,1)} %collective-permute-done.2, bf16[384,1280]{1,0:T(8,128)(2,1)} %collective-permute-done.13) | non-fusion elementwise | flops 491520 | bytes 2949120 | tf_op jit(solution)/shard_map/add | solution.py:221
  157.8 9.4 %collective-permute-done.5 = bf16[96,5120]{1,0:T(8,128)(2,1)S(1)} collective-permute-done((bf16[96,5120]{1,0:T(8,128)(2,1)}, bf16[96,5120]{1,0:T(8,128)(2,1)S(1)}, u32[]{:S(2)}, u32[]{:S(2)}) %collective-permute-start.5) | collective-permute-done | bytes 983072 | tf_op jit(solution)/shard_map/ppermute | solution.py:32
  169.6 4.4 %collective-permute-start.15 = (bf16[2,360,1280]{2,1,0:T(8,128)(2,1)}, bf16[2,360,1280]{2,1,0:T(8,128)(2,1)}, u32[]{:S(2)}, u32[]{:S(2)}) collective-permute-start(bf16[2,360,1280]{2,1,0:T(8,128)(2,1)} %get-tuple-element.58), channel_id=1, source_target_pairs={{0,4},{4,8},{8,12},{12,16},{16,20},{20,24},{24,28},{1,5},{5,9},{9,... | collective-permute-start | bytes 5529608 | tf_op jit(solution)/shard_map/ppermute | solution.py:38
  176.9 3.6 %fusion.21 = f32[1280,640]{1,0:T(8,128)S(1)} fusion(bf16[768,640]{1,0:T(8,128)(2,1)} %bitcast.55, bf16[384,1280]{1,0:T(8,128)(2,1)} %collective-permute-done.25, bf16[384,1280]{1,0:T(8,128)(2,1)} %add.380), kind=kOutput, calls=%fused_computation.23 | convolution fusion | flops 1262223360 | bytes 6225920 | tf_op jit(solution)/shard_map/dot_general | solution.py:27
  180.5 3.3 %fusion.25 = f32[1280,640]{1,0:T(8,128)S(1)} fusion(bf16[768,640]{1,0:T(8,128)(2,1)S(1)} %bitcast.54, bf16[384,1280]{1,0:T(8,128)(2,1)} %collective-permute-done.26, bf16[384,1280]{1,0:T(8,128)(2,1)} %add.382), kind=kOutput, calls=%fused_computation.27 | convolution fusion | flops 1262223360 | bytes 6225920 | tf_op jit(solution)/shard_map/dot_general | solution.py:27
  183.9 3.3 %fusion.17 = f32[1280,640]{1,0:T(8,128)S(1)} fusion(bf16[768,640]{1,0:T(8,128)(2,1)S(1)} %bitcast.53, bf16[384,1280]{1,0:T(8,128)(2,1)} %collective-permute-done.24, bf16[384,1280]{1,0:T(8,128)(2,1)} %add.378), kind=kOutput, calls=%fused_computation.19 | convolution fusion | flops 1262223360 | bytes 6225920 | tf_op jit(solution)/shard_map/dot_general | solution.py:27
  187.3 3.2 %fusion.10 = bf16[1280,640]{1,0:T(8,128)(2,1)} fusion(f32[1280,640]{1,0:T(8,128)S(1)} %fusion.25, f32[1280,640]{1,0:T(8,128)S(1)} %fusion.21, f32[1280,640]{1,0:T(8,128)S(1)} %fusion.17, bf16[768,640]{1,0:T(8,128)(2,1)S(1)} %bitcast.51, bf16[384,1280]{1,0:T(8,128)(2,1)S(1)} %collective-permute-done.16, bf16[384,1280]{1,0:T(8,128)(2,1)S(1)} %get-tuple-element.37), kind=kOutput, calls=%fused_computation.14 | convolution fusion | flops 1265500160 | bytes 14417920 | tf_op jit(solution)/shard_map/dot_general | solution.py:27
  190.4 2.7 %collective-permute-done.14 = bf16[2,360,1280]{2,1,0:T(8,128)(2,1)} collective-permute-done((bf16[2,360,1280]{2,1,0:T(8,128)(2,1)}, bf16[2,360,1280]{2,1,0:T(8,128)(2,1)}, u32[]{:S(2)}, u32[]{:S(2)}) %collective-permute-start.14) | collective-permute-done | bytes 1843232 | tf_op jit(solution)/shard_map/ppermute | solution.py:38
  194.3 4.0 %add_convert_fusion = bf16[2,360,1280]{2,1,0:T(8,128)(2,1)} fusion(bf16[2,360,1280]{2,1,0:T(8,128)(2,1)} %collective-permute-done.15, f32[2,360,1280]{2,1,0:T(8,128)S(1)} %copy-done.7, bf16[2,360,1280]{2,1,0:T(8,128)(2,1)} %collective-permute-done.14), kind=kLoop, calls=%fused_computation.10 | loop fusion | flops 4608000 | bytes 9216000 | tf_op jit(solution)/shard_map/convert_element_type | solution.py:282
  (105 shorter events, 43.1 us)
Async XLA Ops:
  3.7 34.5 %collective-permute-start.9 = (bf16[96,5120]{1,0:T(8,128)(2,1)}, bf16[96,5120]{1,0:T(8,128)(2,1)}, u32[]{:S(2)}, u32[]{:S(2)}) collective-permute-start(bf16[96,5120]{1,0:T(8,128)(2,1)} %pad.8), channel_id=1, source_target_pairs={{0,3},{1,2},{2,1},{3,0},{4,7},{5,6},{6,5},{7,4},{8,11},{9,10},{10,... | collective-permute-start | bytes 2949128 | tf_op jit(solution)/shard_map/ppermute | solution.py:32
  6.7 48.9 %collective-permute-start.8 = (bf16[96,5120]{1,0:T(8,128)(2,1)}, bf16[96,5120]{1,0:T(8,128)(2,1)}, u32[]{:S(2)}, u32[]{:S(2)}) collective-permute-start(bf16[96,5120]{1,0:T(8,128)(2,1)} %pad.8), channel_id=1, source_target_pairs={{0,2},{1,3},{2,0},{3,1},{4,6},{5,7},{6,4},{7,5},{8,10},{9,11},{10,... | collective-permute-start | bytes 2949128 | tf_op jit(solution)/shard_map/ppermute | solution.py:32
  7.0 48.6 %collective-permute-start.7 = (bf16[96,5120]{1,0:T(8,128)(2,1)}, bf16[96,5120]{1,0:T(8,128)(2,1)}, u32[]{:S(2)}, u32[]{:S(2)}) collective-permute-start(bf16[96,5120]{1,0:T(8,128)(2,1)} %pad.8), channel_id=1, source_target_pairs={{0,1},{1,0},{2,3},{3,2},{4,5},{5,4},{6,7},{7,6},{8,9},{9,8},{10,11... | collective-permute-start | bytes 2949128 | tf_op jit(solution)/shard_map/ppermute | solution.py:32
  7.0 26.4 %collective-permute-start.1 = (bf16[2,360,1280]{2,1,0:T(8,128)(2,1)}, bf16[2,360,1280]{2,1,0:T(8,128)(2,1)}, u32[]{:S(2)}, u32[]{:S(2)}) collective-permute-start(bf16[2,360,1280]{2,1,0:T(8,128)(2,1)} %bitcast.1.own_ref.refs_1_), channel_id=1, source_target_pairs={{4,0},{8,4},{12,8},{16,12},{20,16},{24,20},{28,24},{5,1},{9,5},{13... | collective-permute-start | bytes 5529608 | tf_op jit(solution)/shard_map/ppermute | solution.py:38
  10.2 24.1 %collective-permute-start = (bf16[2,360,1280]{2,1,0:T(8,128)(2,1)}, bf16[2,360,1280]{2,1,0:T(8,128)(2,1)}, u32[]{:S(2)}, u32[]{:S(2)}) collective-permute-start(bf16[2,360,1280]{2,1,0:T(8,128)(2,1)} %bitcast.1.own_ref.refs_1_), channel_id=1, source_target_pairs={{0,4},{4,8},{8,12},{12,16},{16,20},{20,24},{24,28},{1,5},{5,9},{9,... | collective-permute-start | bytes 5529608 | tf_op jit(solution)/shard_map/ppermute | solution.py:38
  35.7 24.1 %collective-permute-start.19 = (bf16[96,1280]{1,0:T(8,128)(2,1)S(1)}, bf16[96,1280]{1,0:T(8,128)(2,1)S(1)}, u32[]{:S(2)}, u32[]{:S(2)}) collective-permute-start(bf16[96,1280]{1,0:T(8,128)(2,1)S(1)} %get-tuple-element.85), channel_id=1, source_target_pairs={{0,24},{4,28},{8,0},{12,4},{16,8},{20,12},{24,16},{28,20},{1,25},{... | collective-permute-start | bytes 737288 | tf_op jit(solution)/shard_map/ppermute | solution.py:43
  35.7 24.1 %collective-permute-start.18 = (bf16[96,1280]{1,0:T(8,128)(2,1)S(1)}, bf16[96,1280]{1,0:T(8,128)(2,1)S(1)}, u32[]{:S(2)}, u32[]{:S(2)}) collective-permute-start(bf16[96,1280]{1,0:T(8,128)(2,1)S(1)} %get-tuple-element.86), channel_id=1, source_target_pairs={{0,16},{4,20},{8,24},{12,28},{16,0},{20,4},{24,8},{28,12},{1,17},{... | collective-permute-start | bytes 737288 | tf_op jit(solution)/shard_map/ppermute | solution.py:43
  55.6 26.2 %collective-permute-start.2 = (bf16[384,1280]{1,0:T(8,128)(2,1)S(1)}, bf16[384,1280]{1,0:T(8,128)(2,1)}, u32[]{:S(2)}, u32[]{:S(2)}) collective-permute-start(bf16[384,1280]{1,0:T(8,128)(2,1)S(1)} %get-tuple-element.37), channel_id=1, source_target_pairs={{0,8},{4,12},{8,16},{12,20},{16,24},{20,28},{1,9},{5,13},{9,17},{1... | collective-permute-start | bytes 2949128 | tf_op jit(solution)/shard_map/ppermute | solution.py:38
  58.5 23.3 %collective-permute-start.3 = (bf16[384,1280]{1,0:T(8,128)(2,1)S(1)}, bf16[384,1280]{1,0:T(8,128)(2,1)}, u32[]{:S(2)}, u32[]{:S(2)}) collective-permute-start(bf16[384,1280]{1,0:T(8,128)(2,1)S(1)} %get-tuple-element.37), channel_id=1, source_target_pairs={{8,0},{12,4},{16,8},{20,12},{24,16},{28,20},{9,1},{13,5},{17,9},{2... | collective-permute-start | bytes 2949128 | tf_op jit(solution)/shard_map/ppermute | solution.py:38
  79.1 38.4 %collective-permute-start.22 = (bf16[4,2,96,640]{3,2,0,1:T(8,128)(2,1)S(1)}, bf16[4,2,96,640]{3,2,0,1:T(8,128)(2,1)}, u32[]{:S(2)}, u32[]{:S(2)}) collective-permute-start(bf16[4,2,96,640]{3,2,0,1:T(8,128)(2,1)S(1)} %get-tuple-element.81), channel_id=1, source_target_pairs={{0,2},{1,3},{2,0},{3,1},{4,6},{5,7},{6,4},{7,5},{8,10},{9,11},{10,... | collective-permute-start | bytes 2949128 | tf_op jit(solution)/shard_map/ppermute | solution.py:32
  80.4 37.3 %collective-permute-start.21 = (bf16[4,2,96,640]{3,2,0,1:T(8,128)(2,1)S(1)}, bf16[4,2,96,640]{3,2,0,1:T(8,128)(2,1)}, u32[]{:S(2)}, u32[]{:S(2)}) collective-permute-start(bf16[4,2,96,640]{3,2,0,1:T(8,128)(2,1)S(1)} %get-tuple-element.81), channel_id=1, source_target_pairs={{0,1},{1,0},{2,3},{3,2},{4,5},{5,4},{6,7},{7,6},{8,9},{9,8},{10,11... | collective-permute-start | bytes 2949128 | tf_op jit(solution)/shard_map/ppermute | solution.py:32
  81.6 43.0 %collective-permute-start.23 = (bf16[4,2,96,640]{3,2,0,1:T(8,128)(2,1)S(1)}, bf16[4,2,96,640]{3,2,0,1:T(8,128)(2,1)}, u32[]{:S(2)}, u32[]{:S(2)}) collective-permute-start(bf16[4,2,96,640]{3,2,0,1:T(8,128)(2,1)S(1)} %get-tuple-element.81), channel_id=1, source_target_pairs={{0,3},{1,2},{2,1},{3,0},{4,7},{5,6},{6,5},{7,4},{8,11},{9,10},{10,... | collective-permute-start | bytes 2949128 | tf_op jit(solution)/shard_map/ppermute | solution.py:32
  81.8 33.3 %collective-permute-start.10 = (bf16[384,1280]{1,0:T(8,128)(2,1)}, bf16[384,1280]{1,0:T(8,128)(2,1)}, u32[]{:S(2)}, u32[]{:S(2)}) collective-permute-start(bf16[384,1280]{1,0:T(8,128)(2,1)} %collective-permute-done.2), channel_id=1, source_target_pairs={{0,8},{4,12},{8,16},{12,20},{16,24},{20,28},{1,9},{5,13},{9,17},{1... | collective-permute-start | bytes 2949128 | tf_op jit(solution)/shard_map/ppermute | solution.py:38
  87.2 30.1 %collective-permute-start.11 = (bf16[384,1280]{1,0:T(8,128)(2,1)}, bf16[384,1280]{1,0:T(8,128)(2,1)}, u32[]{:S(2)}, u32[]{:S(2)}) collective-permute-start(bf16[384,1280]{1,0:T(8,128)(2,1)} %collective-permute-done.3), channel_id=1, source_target_pairs={{8,0},{12,4},{16,8},{20,12},{24,16},{28,20},{9,1},{13,5},{17,9},{2... | collective-permute-start | bytes 2949128 | tf_op jit(solution)/shard_map/ppermute | solution.py:38
  115.1 42.3 %collective-permute-start.6 = (bf16[96,5120]{1,0:T(8,128)(2,1)}, bf16[96,5120]{1,0:T(8,128)(2,1)S(1)}, u32[]{:S(2)}, u32[]{:S(2)}) collective-permute-start(bf16[96,5120]{1,0:T(8,128)(2,1)} %get-tuple-element.77), channel_id=1, source_target_pairs={{0,3},{1,2},{2,1},{3,0},{4,7},{5,6},{6,5},{7,4},{8,11},{9,10},{10,... | collective-permute-start | bytes 2949128 | tf_op jit(solution)/shard_map/ppermute | solution.py:32
  117.3 50.0 %collective-permute-start.5 = (bf16[96,5120]{1,0:T(8,128)(2,1)}, bf16[96,5120]{1,0:T(8,128)(2,1)S(1)}, u32[]{:S(2)}, u32[]{:S(2)}) collective-permute-start(bf16[96,5120]{1,0:T(8,128)(2,1)} %get-tuple-element.78), channel_id=1, source_target_pairs={{0,2},{1,3},{2,0},{3,1},{4,6},{5,7},{6,4},{7,5},{8,10},{9,11},{10,... | collective-permute-start | bytes 2949128 | tf_op jit(solution)/shard_map/ppermute | solution.py:32
  117.5 52.1 %collective-permute-start.4 = (bf16[96,5120]{1,0:T(8,128)(2,1)}, bf16[96,5120]{1,0:T(8,128)(2,1)S(1)}, u32[]{:S(2)}, u32[]{:S(2)}) collective-permute-start(bf16[96,5120]{1,0:T(8,128)(2,1)} %get-tuple-element.79), channel_id=1, source_target_pairs={{0,1},{1,0},{2,3},{3,2},{4,5},{5,4},{6,7},{7,6},{8,9},{9,8},{10,11... | collective-permute-start | bytes 2949128 | tf_op jit(solution)/shard_map/ppermute | solution.py:32
  117.7 32.3 %collective-permute-start.12 = (bf16[384,1280]{1,0:T(8,128)(2,1)}, bf16[384,1280]{1,0:T(8,128)(2,1)}, u32[]{:S(2)}, u32[]{:S(2)}) collective-permute-start(bf16[384,1280]{1,0:T(8,128)(2,1)} %collective-permute-done.10), channel_id=1, source_target_pairs={{0,8},{4,12},{8,16},{12,20},{16,24},{20,28},{1,9},{5,13},{9,17},{1... | collective-permute-start | bytes 2949128 | tf_op jit(solution)/shard_map/ppermute | solution.py:38
  124.6 30.0 %collective-permute-start.13 = (bf16[384,1280]{1,0:T(8,128)(2,1)}, bf16[384,1280]{1,0:T(8,128)(2,1)}, u32[]{:S(2)}, u32[]{:S(2)}) collective-permute-start(bf16[384,1280]{1,0:T(8,128)(2,1)} %collective-permute-done.11), channel_id=1, source_target_pairs={{8,0},{12,4},{16,8},{20,12},{24,16},{28,20},{9,1},{13,5},{17,9},{2... | collective-permute-start | bytes 2949128 | tf_op jit(solution)/shard_map/ppermute | solution.py:38
  150.0 26.8 %collective-permute-start.25 = (bf16[384,1280]{1,0:T(8,128)(2,1)}, bf16[384,1280]{1,0:T(8,128)(2,1)}, u32[]{:S(2)}, u32[]{:S(2)}) collective-permute-start(bf16[384,1280]{1,0:T(8,128)(2,1)} %add.380), channel_id=1, source_target_pairs={{0,4},{4,0},{8,12},{12,8},{16,20},{20,16},{24,28},{28,24},{1,5},{5... | collective-permute-start | bytes 2949128 | tf_op jit(solution)/shard_map/ppermute | solution.py:32
  154.6 25.9 %collective-permute-start.26 = (bf16[384,1280]{1,0:T(8,128)(2,1)}, bf16[384,1280]{1,0:T(8,128)(2,1)}, u32[]{:S(2)}, u32[]{:S(2)}) collective-permute-start(bf16[384,1280]{1,0:T(8,128)(2,1)} %add.382), channel_id=1, source_target_pairs={{0,4},{4,0},{8,12},{12,8},{16,20},{20,16},{24,28},{28,24},{1,5},{5... | collective-permute-start | bytes 2949128 | tf_op jit(solution)/shard_map/ppermute | solution.py:32
  157.3 26.5 %collective-permute-start.24 = (bf16[384,1280]{1,0:T(8,128)(2,1)}, bf16[384,1280]{1,0:T(8,128)(2,1)}, u32[]{:S(2)}, u32[]{:S(2)}) collective-permute-start(bf16[384,1280]{1,0:T(8,128)(2,1)} %add.378), channel_id=1, source_target_pairs={{0,4},{4,0},{8,12},{12,8},{16,20},{20,16},{24,28},{28,24},{1,5},{5... | collective-permute-start | bytes 2949128 | tf_op jit(solution)/shard_map/ppermute | solution.py:32
  167.2 25.9 %collective-permute-start.14 = (bf16[2,360,1280]{2,1,0:T(8,128)(2,1)}, bf16[2,360,1280]{2,1,0:T(8,128)(2,1)}, u32[]{:S(2)}, u32[]{:S(2)}) collective-permute-start(bf16[2,360,1280]{2,1,0:T(8,128)(2,1)} %get-tuple-element.57), channel_id=1, source_target_pairs={{4,0},{8,4},{12,8},{16,12},{20,16},{24,20},{28,24},{5,1},{9,5},{13... | collective-permute-start | bytes 5529608 | tf_op jit(solution)/shard_map/ppermute | solution.py:38
  169.6 24.7 %collective-permute-start.15 = (bf16[2,360,1280]{2,1,0:T(8,128)(2,1)}, bf16[2,360,1280]{2,1,0:T(8,128)(2,1)}, u32[]{:S(2)}, u32[]{:S(2)}) collective-permute-start(bf16[2,360,1280]{2,1,0:T(8,128)(2,1)} %get-tuple-element.58), channel_id=1, source_target_pairs={{0,4},{4,8},{8,12},{12,16},{16,20},{20,24},{24,28},{1,5},{5,9},{9,... | collective-permute-start | bytes 5529608 | tf_op jit(solution)/shard_map/ppermute | solution.py:38
  (14 other events, 168.4 us)
